TPU v7x, 32 devices: a whole 2x2x4 slice. The times are simulated.
32 devices in a mesh: row: 8 (over z, core), col: 4 (over y, x).
Axes of the slice: x: 2, y: 2, z: 4, core: 2. Of those that a mesh axis runs over, the one named last changes fastest.
Arguments:
- amplitudes: bfloat16 [4096, 4096], P('row', 'col'), may hold values from -6 to 6
- integrals: bfloat16 [4096, 4096], P('col', 'row'), may hold values from -0.125 to 0.125
- amp_occupancy: int32 [32, 32], P('row', 'col'), may hold values 0 or 1
- int_occupancy: int32 [32, 32], P('col', 'row'), may hold values 0 or 1
- owner_map: int32 [32], replicated, may hold values from 0 to 31, each once
Outputs:
- residual: bfloat16 [4096, 4096], P('row', 'col')
Inputs may be any that keep to these rules, and one draw needn't show every extreme that they name: `owner_map`: each tile number appears once.
All inputs are finite; a program needn't handle non-finite values. No bound on the sum of `amp_occupancy` or of `int_occupancy` on one device may be relied on, other than what follows from the above.
Results may differ from a plain program's by a relative error of at most 0.014.
Values may be sent and summed in bfloat16 or wider, within the bound.
A program may use at most 64 MiB of HBM per device.

v0:
```python
import jax
import jax.numpy as jnp
from jax import lax
from jax.sharding import PartitionSpec as P

TILE = 128
NJ = 4096


def mask_tiles(matrix, occupancy):
    nrow, ncolumn = matrix.shape
    blocks = matrix.reshape(nrow // TILE, TILE, ncolumn // TILE, TILE)
    return (blocks * occupancy[:, None, :, None].astype(jnp.bfloat16)).reshape(nrow, ncolumn)


def on_device(amplitudes, integrals, amp_occupancy, int_occupancy, owner_map):
    masked_amp = mask_tiles(amplitudes, amp_occupancy)
    masked_int = mask_tiles(integrals, int_occupancy)
    nrow, kloc = masked_amp.shape
    tiles_all = NJ // TILE
    partial_value = jnp.dot(
        masked_amp,
        lax.all_gather(masked_int, "row", axis=1, tiled=True),
        preferred_element_type=jnp.float32,
    )
    ordered = partial_value.reshape(nrow, tiles_all, TILE)[:, owner_map, :].reshape(nrow, NJ)
    summed = lax.psum_scatter(ordered.astype(jnp.bfloat16), "col", scatter_dimension=1, tiled=True)
    return summed


def solution(mesh):
    placed = (P("row", "col"), P("col", "row"), P("row", "col"), P("col", "row"), P())
    return jax.shard_map(
        on_device, mesh=mesh, in_specs=placed, out_specs=P("row", "col"), check_vma=False
    )
```

profile of v0, /device:TPU:0, one launch (start us, length us, event | category | flops | bytes accessed | tf_op | source)
XLA Modules:
  0.0 187.8 jit_solution(14628121612643449842)
XLA Ops:
  6.5 0.0 copy-start
  6.5 0.0 copy-start.2
  6.5 0.0 all-gather.2.cloned.1.call-start
  6.5 0.7 convert_element_type.15
  7.3 0.1 copy.8
  7.3 0.3 mul.25
  7.7 2.3 %bitcast_multiply_fusion = bf16[1024,512]{1,0:T(8,128)(2,1)} fusion(bf16[1024,512]{1,0:T(8,128)(2,1)} %param.6, bf16[128,8,4,128]{3,2,1,0:T(4,128)(2,1)S(1)} %bitcast.25), kind=kLoop, calls=%fused_computation.2 | loop fusion | flops 524288 | bytes 3145728 | tf_op jit(solution)/shard_map/mul | solution.py:13
  10.0 0.0 all-gather.2.cloned.1.call-update
  10.1 0.0 reduce-scatter.2.cloned.1.call-start
  10.1 0.0 copy-done
  10.1 0.0 copy-done.2
  10.2 84.8 %all-gather.2.cloned.1.call-done = bf16[1024,4096]{1,0:T(8,128)(2,1)} async-done(((bf16[1024,512]{1,0:T(8,128)(2,1)}), bf16[1024,4096]{1,0:T(8,128)(2,1)}) %all-gather.2.cloned.1.call-update) | async-done | bytes 8388624 | tf_op jit(solution)/shard_map/all_gather | solution.py:23
  95.0 0.0 copy-start.1
  95.0 12.1 %copy.9 = bf16[4096,1024]{1,0:T(8,128)(2,1)} copy(bf16[4096,1024]{0,1:T(8,128)(2,1)} %bitcast.23) | data formatting | bytes 16777216 | tf_op jit(solution)/shard_map/dot_general | solution.py:21
  107.1 0.2 mul.22
  107.3 0.0 copy-done.1
  107.3 8.3 %fusion.1 = bf16[512,32,128]{2,0,1:T(8,128)(2,1)} fusion(bf16[32,128,1024]{2,1,0:T(8,128)(2,1)} %bitcast.24, bf16[512,1024]{1,0:T(8,128)(2,1)S(1)} %copy-done.1, bf16[64,8,8,128]{3,2,1,0:T(8,128)(2,1)S(1)} %bitcast.26), kind=kOutput, calls=%fused_computation.5 | convolution fusion | flops 4297064448 | bytes 14680064 | tf_op jit(solution)/shard_map/dot_general | solution.py:21
  115.6 5.2 %gather_fusion = bf16[32,512,128]{2,1,0:T(8,128)(2,1)} fusion(bf16[512,32,128]{2,0,1:T(8,128)(2,1)} %fusion.1, s32[1024]{0:T(1024)S(1)} %pad_clamp_fusion), kind=kCustom, calls=%fused_computation | custom fusion | bytes 8388736 | tf_op jit(solution)/shard_map/gather | solution.py:26
  120.8 6.5 %copy.10 = bf16[512,32,128]{0,2,1:T(8,128)(2,1)} copy(bf16[512,32,128]{2,0,1:T(8,128)(2,1)} %bitcast.22) | data formatting | bytes 8388608 | tf_op jit(solution)/shard_map/convert_element_type | solution.py:27
  127.3 0.0 reduce-scatter.2.cloned.1.call-update
  127.3 51.4 %reduce-scatter.2.cloned.1.call-done = bf16[512,1024]{0,1:T(8,128)(2,1)} async-done(((bf16[512,4096]{0,1:T(8,128)(2,1)}), bf16[512,1024]{0,1:T(8,128)(2,1)}) %reduce-scatter.2.cloned.1.call-update) | async-done | bytes 1048592 | tf_op jit(solution)/shard_map/reduce_scatter | solution.py:27
  178.7 2.3 %copy.11 = bf16[512,1024]{1,0:T(8,128)(2,1)} copy(bf16[512,1024]{0,1:T(8,128)(2,1)} %reduce-scatter.2.cloned.1.call-done) | data formatting | bytes 2097152 | tf_op jit(solution)/shard_map/reduce_scatter | solution.py:27
  (3 shorter events, 0.0 us)
Async XLA Ops:
  6.5 3.6 %copy-start = (s32[4,8]{1,0:T(4,128)S(1)}, s32[4,8]{1,0:T(4,128)}, u32[]{:S(2)}) copy-start(s32[4,8]{1,0:T(4,128)} %param.7) | copy-start | bytes 388
  6.5 3.6 %copy-start.2 = (s32[32]{0:T(128)S(1)}, s32[32]{0:T(128)}, u32[]{:S(2)}) copy-start(s32[32]{0:T(128)} %param.9) | copy-start | bytes 388
  6.5 88.4 %all-gather.2.cloned.1.call-start = ((), (), s32[]{:S(2)}) async-start(), calls=%async_computation.1 | async-start | bytes 9437184 | tf_op jit(solution)/shard_map/all_gather | solution.py:23
  10.1 168.7 %reduce-scatter.2.cloned.1.call-start = ((), (), s32[]{:S(2)}) async-start(), calls=%async_computation.2 | async-start | bytes 5242880 | tf_op jit(solution)/shard_map/reduce_scatter | solution.py:27
  95.0 12.3 %copy-start.1 = (bf16[512,1024]{1,0:T(8,128)(2,1)S(1)}, bf16[512,1024]{1,0:T(8,128)(2,1)}, u32[]{:S(2)}) copy-start(bf16[512,1024]{1,0:T(8,128)(2,1)} %param.5) | copy-start | bytes 3145732
Sparse Core Ops, SparseCore 0:
  10.2 84.7 all-gather.1
  127.5 51.2 reduce-scatter.1
where the time goes:
time: 188 us
  waiting for transfers between devices  136 us (72%)
  local copies, waits for them, and re-layouts  26.7 us (14%)
  between operations  13.5 us (7%)
  matrix products  8.32 us (4%)
  other arithmetic  3.07 us (2%)
    all_gather x1, waiting for transfers between devices, on_device(): lax.all_gather(masked_int, 'row', axis=1, tiled=True)  84.8 us
    reduce_scatter x1, waiting for transfers between devices, on_device(): lax.psum_scatter(ordered.astype(jnp.bfloat16), 'col', scatter_dimension=1...  51.4 us
    dot_general x1, local copies, waits for them, and re-layouts, on_device(): jnp.dot(masked_amp, lax.all_gather(masked_int, 'row', axis=1, tiled=True)...  12.1 us
    dot_general x1, matrix products, on_device(): jnp.dot(masked_amp, lax.all_gather(masked_int, 'row', axis=1, tiled=True)...  8.32 us
    convert_element_type x1, local copies, waits for them, and re-layouts, on_device(): ordered.astype(jnp.bfloat16)  6.5 us
    gather x1, local copies, waits for them, and re-layouts, on_device(): partial_value.reshape(nrow, tiles_all, TILE)[:, owner_map, :]  5.21 us
  transfers between devices with their start and end apart: 2, of which 2 were waited for; matrix products, arithmetic and copies ran while one was open for 0% of the time, Pallas kernels for 0%

commit v1 on v0

v1 whole, which is shorter than its diff:
```python
import functools

import jax
import jax.numpy as jnp
from jax import lax
from jax.experimental import pallas as pl
from jax.experimental.pallas import tpu as pltpu
from jax.sharding import PartitionSpec as P

TILE = 128
CORES = 2
MESH = pl.DeviceIdType.MESH


def flip(value, mask):
    bit, out = 1, value
    while bit <= mask:
        if mask & bit:
            out = out + bit - 2 * bit * (lax.rem(value // bit, 2))
        bit *= 2
    return out


def orders(ncol):
    bits = [1 << i for i in range(ncol.bit_length() - 1)]
    return (bits, bits[::-1])


def first_stage(offset, order):
    for stage, bit in enumerate(order):
        if offset & bit:
            return stage
    return None


def kernel(nrow, ncol, amp_occ, int_occ, owner, amp, integ, out,
           masked, gath, part, landed, recv, right_send, left_send, twin_send, col_send, col_recv):
    nz = nrow // CORES
    row, col = lax.axis_index("row"), lax.axis_index("col")
    z, core = row // CORES, lax.rem(row, CORES)
    twin = z * CORES + (CORES - 1) - core
    has_left, has_right = z > 0, z < nz - 1
    tiles = integ.shape[1] // TILE
    ktiles = integ.shape[0] // TILE
    nrows = amp.shape[0]
    half = nrows // 2
    width = out.shape[1]
    per_col = width // TILE
    order = orders(ncol)

    barrier = pltpu.get_barrier_semaphore()
    pl.semaphore_signal(barrier, inc=1, device_id={"row": twin}, device_id_type=MESH)
    for bit in order[0]:
        pl.semaphore_signal(barrier, inc=1, device_id={"col": flip(col, bit)}, device_id_type=MESH)

    @pl.when(has_left)
    def _():
        pl.semaphore_signal(barrier, inc=1, device_id={"row": row - CORES}, device_id_type=MESH)

    @pl.when(has_right)
    def _():
        pl.semaphore_signal(barrier, inc=1, device_id={"row": row + CORES}, device_id_type=MESH)

    def mask_int(j):
        for k in range(ktiles):
            scale = int_occ[k, j].astype(jnp.float32)
            block = integ[k * TILE:(k + 1) * TILE, j * TILE:(j + 1) * TILE].astype(jnp.float32) * scale
            gath[row * tiles + j, k * TILE:(k + 1) * TILE, :] = block.astype(jnp.bfloat16)

    mask_int(0)
    pl.semaphore_wait(barrier, 1 + len(order[0]) + has_left.astype(jnp.int32) + has_right.astype(jnp.int32))

    def hop(tile, send, target):
        return pltpu.make_async_remote_copy(
            src_ref=gath.at[tile], dst_ref=gath.at[tile], send_sem=send.at[tile],
            recv_sem=recv.at[tile], device_id={"row": target}, device_id_type=MESH)

    for j in range(tiles):
        if j > 0:
            mask_int(j)
        mine = row * tiles + j

        @pl.when(has_right)
        def _():
            hop(mine, right_send, row + CORES).start()

        @pl.when(has_left)
        def _():
            hop(mine, left_send, row - CORES).start()

        hop(mine, twin_send, twin).start()

    for i in range(nrows // TILE):
        for k in range(ktiles):
            scale = amp_occ[i, k].astype(jnp.float32)
            block = amp[i * TILE:(i + 1) * TILE, k * TILE:(k + 1) * TILE].astype(jnp.float32) * scale
            masked[i * TILE:(i + 1) * TILE, k * TILE:(k + 1) * TILE] = block.astype(jnp.bfloat16)

    for step in range(1, nz):
        for j in range(tiles):
            from_left = ((z - step) * CORES + core) * tiles + j
            from_right = ((z + step) * CORES + core) * tiles + j

            @pl.when(z >= step)
            def _():
                hop(from_left, right_send, twin).wait_recv()

                @pl.when(has_right)
                def _():
                    hop(from_left, right_send, row + CORES).start()

                hop(from_left, twin_send, twin).start()

            @pl.when(z + step < nz)
            def _():
                hop(from_right, left_send, twin).wait_recv()

                @pl.when(has_left)
                def _():
                    hop(from_right, left_send, row - CORES).start()

                hop(from_right, twin_send, twin).start()

    for other in range(nz):
        for j in range(tiles):
            hop((other * CORES + (CORES - 1) - core) * tiles + j, twin_send, twin).wait_recv()

    pair = 2 if per_col % 2 == 0 else 1

    def multiply(offset):
        base = flip(col, offset) * per_col

        @pl.loop(0, per_col // pair)
        def _(i):
            right = [gath[owner[base + i * pair + p]] for p in range(pair)]
            right = right[0] if pair == 1 else jnp.concatenate(right, axis=1)
            value = jnp.dot(masked[...], right, preferred_element_type=jnp.float32)
            at = pl.multiple_of(i * pair * TILE, pair * TILE)
            part[offset, :, pl.ds(at, pair * TILE)] = value.astype(jnp.bfloat16)

    slot = {}
    for h in range(2):
        for stage in range(len(order[h])):
            for offset in range(ncol):
                if not any(offset & bit for bit in order[h][:stage + 1]):
                    slot[h, stage, offset] = len(slot)

    def reduce_hop(h, offset):
        stage = first_stage(offset, order[h])
        bit = order[h][stage]
        there = slot[h, stage, offset ^ bit]
        return pltpu.make_async_remote_copy(
            src_ref=part.at[offset, pl.ds(h * half, half), :], dst_ref=landed.at[there],
            send_sem=col_send.at[there], recv_sem=col_recv.at[there],
            device_id={"col": flip(col, bit)}, device_id_type=MESH)

    def total(h, stages, offset):
        value = part[offset, h * half:(h + 1) * half, :].astype(jnp.float32)
        for stage in range(stages):
            value += landed[slot[h, stage, offset]].astype(jnp.float32)
        return value.astype(jnp.bfloat16)

    def arrived(h, stage, offset):
        reduce_hop(h, offset ^ order[h][stage]).wait_recv()

    for offset in range(ncol - 1, -1, -1):
        multiply(offset)
        for h in range(2):
            if first_stage(offset, order[h]) == 0:
                reduce_hop(h, offset).start()
    for stage in range(1, len(order[0])):
        for h in range(2):
            for offset in range(ncol - 1, 0, -1):
                if first_stage(offset, order[h]) == stage:
                    for before in range(stage):
                        arrived(h, before, offset)
                    part[offset, h * half:(h + 1) * half, :] = total(h, stage, offset)
                    reduce_hop(h, offset).start()
    for h in range(2):
        for stage in range(len(order[h])):
            arrived(h, stage, 0)
        out[h * half:(h + 1) * half, :] = total(h, len(order[h]), 0)

    for h in range(2):
        for offset in range(1, ncol):
            reduce_hop(h, offset).wait_send()
    for other in range(nz):
        for j in range(tiles):
            tile = (other * CORES + core) * tiles + j
            hop(tile, twin_send, twin).wait_send()

            @pl.when(has_right & (other <= z))
            def _():
                hop(tile, right_send, twin).wait_send()

            @pl.when(has_left & (other >= z))
            def _():
                hop(tile, left_send, twin).wait_send()


def on_device(nrow, ncol, amplitudes, integrals, amp_occupancy, int_occupancy, owner_map):
    rows, depth = amplitudes.shape
    tiles_all = nrow * integrals.shape[1] // TILE
    width = tiles_all * TILE // ncol
    vmem = pl.BlockSpec(memory_space=pltpu.VMEM)
    smem = pl.BlockSpec(memory_space=pltpu.SMEM)
    slots = 2 * (ncol - 1)
    return pl.pallas_call(
        functools.partial(kernel, nrow, ncol),
        out_shape=jax.ShapeDtypeStruct((rows, width), jnp.bfloat16),
        in_specs=[smem, smem, smem, vmem, vmem],
        out_specs=vmem,
        scratch_shapes=[
            pltpu.VMEM((rows, depth), jnp.bfloat16),
            pltpu.VMEM((tiles_all, depth, TILE), jnp.bfloat16),
            pltpu.VMEM((ncol, rows, width), jnp.bfloat16),
            pltpu.VMEM((slots, rows // 2, width), jnp.bfloat16),
            pltpu.SemaphoreType.DMA((tiles_all,)),
            pltpu.SemaphoreType.DMA((tiles_all,)),
            pltpu.SemaphoreType.DMA((tiles_all,)),
            pltpu.SemaphoreType.DMA((tiles_all,)),
            pltpu.SemaphoreType.DMA((slots,)),
            pltpu.SemaphoreType.DMA((slots,)),
        ],
        compiler_params=pltpu.CompilerParams(
            collective_id=0, has_side_effects=True, vmem_limit_bytes=48 * 1024 * 1024),
        cost_estimate=pl.CostEstimate(
            flops=2 * rows * depth * tiles_all * TILE, bytes_accessed=4 * rows * depth * 2, transcendentals=0),
    )(amp_occupancy, int_occupancy, owner_map, amplitudes, integrals)


def solution(mesh):
    placed = (P("row", "col"), P("col", "row"), P("row", "col"), P("col", "row"), P())
    body = functools.partial(on_device, mesh.shape["row"], mesh.shape["col"])
    return jax.shard_map(body, mesh=mesh, in_specs=placed, out_specs=P("row", "col"), check_vma=False)
```

time: 188 us -> 117 us (0.62)
  waiting for transfers between devices: 136 us -> 0 us
  Pallas kernels: 0 us -> 113 us
  local copies, waits for them, and re-layouts: 26.7 us -> 4.21 us
  between operations: 13.5 us -> 0.01 us
  matrix products: 8.32 us -> 0 us
  other arithmetic: 3.07 us -> 0 us
    pallas_call x0 -> x1, Pallas kernels: none -> 113 us  [on_device(): pl.pallas_call(functools.partial(kernel, nrow, ncol), out_shape=jax.Shape...]
    all_gather x1 -> x0, waiting for transfers between devices: 84.8 us -> none  [on_device(): lax.all_gather(masked_int, 'row', axis=1, tiled=True)]
    reduce_scatter x1 -> x0, waiting for transfers between devices: 51.4 us -> none  [on_device(): lax.psum_scatter(ordered.astype(jnp.bfloat16), 'col', scatter_dimension=1...]
    dot_general x1 -> x0, local copies, waits for them, and re-layouts: 12.1 us -> none  [on_device(): jnp.dot(masked_amp, lax.all_gather(masked_int, 'row', axis=1, tiled=True)...]
    dot_general x1 -> x0, matrix products: 8.32 us -> none  [on_device(): jnp.dot(masked_amp, lax.all_gather(masked_int, 'row', axis=1, tiled=True)...]
    convert_element_type x2 -> x0, local copies, waits for them, and re-layouts: 6.6 us -> none  [the longest x1 6.5 us: on_device(): ordered.astype(jnp.bfloat16)]
    gather x1 -> x0, local copies, waits for them, and re-layouts: 5.21 us -> none  [on_device(): partial_value.reshape(nrow, tiles_all, TILE)[:, owner_map, :]]
    unnamed x6 -> x10, local copies, waits for them, and re-layouts: 0.01 us -> 4.21 us
  transfers between devices with their start and end apart: 2 -> 0, of which waited for: 2 -> 0; matrix products, arithmetic and copies ran while one was open for 0% -> 0% of each run, Pallas kernels for 0% -> 0%
where the time goes in v1:
time: 117 us
  Pallas kernels  113 us (97%)
  local copies, waits for them, and re-layouts  4.21 us (4%)
    pallas_call x1, Pallas kernels, on_device(): pl.pallas_call(functools.partial(kernel, nrow, ncol), out_shape=jax.Shape...  113 us
    unnamed x10, local copies, waits for them, and re-layouts  4.21 us

profile of v1, /device:TPU:0, one launch (start us, length us, event | category | flops | bytes accessed | tf_op | source)
XLA Modules:
  0.0 116.8 jit_solution(2431704887011846253)
XLA Ops:
  0.0 0.0 copy-start.3
  0.0 0.0 copy-start.2
  0.0 0.8 copy.6.int_occ
  0.8 0.0 copy-done.3
  0.8 0.0 copy-done.2
  0.8 0.0 copy-start
  0.8 1.2 %copy-done = bf16[512,1024]{1,0:T(8,128)(2,1)S(1)} copy-done((bf16[512,1024]{1,0:T(8,128)(2,1)S(1)}, bf16[512,1024]{1,0:T(8,128)(2,1)}, u32[]{:S(2)}) %copy-start) | copy-done | bytes 1048600
  2.0 0.0 copy-start.1
  2.0 1.2 %copy-done.1 = bf16[1024,512]{1,0:T(8,128)(2,1)S(1)} copy-done((bf16[1024,512]{1,0:T(8,128)(2,1)S(1)}, bf16[1024,512]{1,0:T(8,128)(2,1)}, u32[]{:S(2)}) %copy-start.1) | copy-done | bytes 1048600
  3.2 112.6 %shard_map.55 = bf16[512,1024]{1,0:T(8,128)(2,1)S(1)} custom-call(s32[4,8]{1,0:T(4,128)S(1)} %copy-done.2, s32[8,4]{1,0:T(8,128)S(1)} %copy.6.int_occ, s32[32]{0:T(128)S(1)} %copy-done.3, bf16[512,1024]{1,0:T(8,128)(2,1)S(1)} %copy-done, bf16[1024,512]{1,0:T(8,128)(2,1)S(1)} %copy-done.1), custom_call_target="tpu_custom_call" | custom-call | flops 4294967296 | bytes 4194304 | tf_op jit(solution)/shard_map/pallas_call | solution.py:208
  115.8 1.0 copy.8
Async XLA Ops:
  0.0 0.8 copy-start.3
  0.0 0.8 copy-start.2
  0.8 1.2 %copy-start = (bf16[512,1024]{1,0:T(8,128)(2,1)S(1)}, bf16[512,1024]{1,0:T(8,128)(2,1)}, u32[]{:S(2)}) copy-start(bf16[512,1024]{1,0:T(8,128)(2,1)} %amp.1) | copy-start | bytes 3145732
  2.0 1.2 %copy-start.1 = (bf16[1024,512]{1,0:T(8,128)(2,1)S(1)}, bf16[1024,512]{1,0:T(8,128)(2,1)}, u32[]{:S(2)}) copy-start(bf16[1024,512]{1,0:T(8,128)(2,1)} %integ.1) | copy-start | bytes 3145732

commit v2 on v1

v2 whole, which is shorter than its diff:
```python
import functools

import jax
import jax.numpy as jnp
from jax import lax
from jax.experimental import pallas as pl
from jax.experimental.pallas import tpu as pltpu
from jax.sharding import PartitionSpec as P

TILE = 128
CORES = 2
LAG = 2
MESH = pl.DeviceIdType.MESH


def flip(value, mask):
    bit, out = 1, value
    while bit <= mask:
        if mask & bit:
            out = out + bit - 2 * bit * (lax.rem(value // bit, 2))
        bit *= 2
    return out


def orders(ncol):
    bits = [1 << i for i in range(ncol.bit_length() - 1)]
    return (bits, bits[::-1])


def kernel(nrow, ncol, amp_occ, int_occ, owner, amp, integ, out,
           masked, gath, part, landed, full, recv, right_send, left_send, twin_send,
           down_send, down_recv, up_send, up_recv):
    nz = nrow // CORES
    row, col = lax.axis_index("row"), lax.axis_index("col")
    z, core = row // CORES, lax.rem(row, CORES)
    twin = z * CORES + (CORES - 1) - core
    has_left, has_right = z > 0, z < nz - 1
    tiles = integ.shape[1] // TILE
    ktiles = integ.shape[0] // TILE
    nrows = amp.shape[0]
    width = out.shape[1]
    per_col = width // TILE
    order = orders(ncol)

    barrier = pltpu.get_barrier_semaphore()
    pl.semaphore_signal(barrier, inc=1, device_id={"row": twin}, device_id_type=MESH)
    for bit in order[0]:
        pl.semaphore_signal(barrier, inc=1, device_id={"col": flip(col, bit)}, device_id_type=MESH)

    @pl.when(has_left)
    def _():
        pl.semaphore_signal(barrier, inc=1, device_id={"row": row - CORES}, device_id_type=MESH)

    @pl.when(has_right)
    def _():
        pl.semaphore_signal(barrier, inc=1, device_id={"row": row + CORES}, device_id_type=MESH)

    def mask_int(j):
        for k in range(ktiles):
            scale = int_occ[k, j].astype(jnp.float32)
            block = integ[k * TILE:(k + 1) * TILE, j * TILE:(j + 1) * TILE].astype(jnp.float32) * scale
            gath[row * tiles + j, k * TILE:(k + 1) * TILE, :] = block.astype(jnp.bfloat16)

    mask_int(0)
    pl.semaphore_wait(barrier, 1 + len(order[0]) + has_left.astype(jnp.int32) + has_right.astype(jnp.int32))

    def hop(tile, send, target):
        return pltpu.make_async_remote_copy(
            src_ref=gath.at[tile], dst_ref=gath.at[tile], send_sem=send.at[tile],
            recv_sem=recv.at[tile], device_id={"row": target}, device_id_type=MESH)

    for j in range(tiles):
        if j > 0:
            mask_int(j)
        mine = row * tiles + j

        @pl.when(has_right)
        def _():
            hop(mine, right_send, row + CORES).start()

        @pl.when(has_left)
        def _():
            hop(mine, left_send, row - CORES).start()

        hop(mine, twin_send, twin).start()

    for i in range(nrows // TILE):
        for k in range(ktiles):
            scale = amp_occ[i, k].astype(jnp.float32)
            block = amp[i * TILE:(i + 1) * TILE, k * TILE:(k + 1) * TILE].astype(jnp.float32) * scale
            masked[i * TILE:(i + 1) * TILE, k * TILE:(k + 1) * TILE] = block.astype(jnp.bfloat16)

    levels = len(order[0])
    units = (nz - 1) * tiles

    def low(h, level):
        at = 0
        for k in range(level):
            at = at + lax.rem(col // order[h][k], 2) * (nrows >> (k + 1))
        return at

    def span(h, level):
        return pl.ds(pl.multiple_of(low(h, level), nrows >> level), nrows >> level)

    def slot(level):
        return pl.ds(nrows - (nrows >> level), nrows >> (level + 1))

    def down(h, level, tile):
        size = nrows >> (level + 1)
        start = low(h, level) + (1 - lax.rem(col // order[h][level], 2)) * size
        return pltpu.make_async_remote_copy(
            src_ref=part.at[tile, pl.ds(pl.multiple_of(start, size), size), :],
            dst_ref=landed.at[tile, slot(level), :],
            send_sem=down_send.at[tile, level], recv_sem=down_recv.at[tile, level],
            device_id={"col": flip(col, order[h][level])}, device_id_type=MESH)

    def up(h, level, tile):
        return pltpu.make_async_remote_copy(
            src_ref=full.at[tile, span(h, level + 1), :], dst_ref=full.at[tile, span(h, level + 1), :],
            send_sem=up_send.at[tile, level], recv_sem=up_recv.at[tile, level],
            device_id={"col": flip(col, order[h][level])}, device_id_type=MESH)

    def multiply(block, j):
        pair = [(block * CORES + c) * tiles + j for c in range(CORES)]
        hop((block * CORES + (CORES - 1) - core) * tiles + j, twin_send, twin).wait_recv()
        right = jnp.concatenate([gath[tile] for tile in pair], axis=1)
        value = jnp.dot(masked[...], right, preferred_element_type=jnp.float32).astype(jnp.bfloat16)
        for h, tile in enumerate(pair):
            part[tile] = value[:, h * TILE:(h + 1) * TILE]
            down(h, 0, tile).start()

    def advance(stage, block, j):
        for h in range(CORES):
            tile = (block * CORES + h) * tiles + j
            if stage < levels:
                down(h, stage, tile).wait_recv()
                keep = span(h, stage + 1)
                value = part[tile, keep, :].astype(jnp.float32) + landed[tile, slot(stage), :].astype(jnp.float32)
                if stage < levels - 1:
                    part[tile, keep, :] = value.astype(jnp.bfloat16)
                    down(h, stage + 1, tile).start()
                else:
                    full[tile, keep, :] = value.astype(jnp.bfloat16)
                    up(h, stage, tile).start()
            else:
                level = 2 * levels - 1 - stage
                up(h, level, tile).wait_recv()
                if level > 0:
                    up(h, level - 1, tile).start()

    def sides(n, lag, action):
        at = n - lag
        step, j = 1 + at // tiles, lax.rem(at, tiles)
        inside = (at >= 0) & (at < units)

        @pl.when((at >= 0) & (at < tiles))
        def _():
            action(z, at)

        @pl.when(inside & (z - step >= 0))
        def _():
            action(z - step, j)

        @pl.when(inside & (z + step < nz))
        def _():
            action(z + step, j)

    def forward(n):
        step, j = 1 + n // tiles, lax.rem(n, tiles)
        from_left = ((z - step) * CORES + core) * tiles + j
        from_right = ((z + step) * CORES + core) * tiles + j

        @pl.when((n < units) & (z - step >= 0))
        def _():
            hop(from_left, right_send, twin).wait_recv()

            @pl.when(has_right)
            def _():
                hop(from_left, right_send, row + CORES).start()

            hop(from_left, twin_send, twin).start()

        @pl.when((n < units) & (z + step < nz))
        def _():
            hop(from_right, left_send, twin).wait_recv()

            @pl.when(has_left)
            def _():
                hop(from_right, left_send, row - CORES).start()

            hop(from_right, twin_send, twin).start()

    @pl.loop(0, units + LAG * 2 * levels + 1)
    def _(n):
        forward(n)
        sides(n, 0, multiply)
        for stage in range(2 * levels):
            sides(n, LAG * (stage + 1), functools.partial(advance, stage))

    for t in range(per_col):
        out[:, t * TILE:(t + 1) * TILE] = full[owner[col * per_col + t]]

    @pl.loop(0, nz * tiles)
    def _(n):
        other, j = n // tiles, lax.rem(n, tiles)
        for h in range(CORES):
            tile = (other * CORES + h) * tiles + j
            for level in range(levels):
                down(h, level, tile).wait_send()
                up(h, level, tile).wait_send()
        mine = (other * CORES + core) * tiles + j
        hop(mine, twin_send, twin).wait_send()

        @pl.when(has_right & (other <= z))
        def _():
            hop(mine, right_send, twin).wait_send()

        @pl.when(has_left & (other >= z))
        def _():
            hop(mine, left_send, twin).wait_send()


def on_device(nrow, ncol, amplitudes, integrals, amp_occupancy, int_occupancy, owner_map):
    rows, depth = amplitudes.shape
    tiles_all = nrow * integrals.shape[1] // TILE
    width = tiles_all * TILE // ncol
    vmem = pl.BlockSpec(memory_space=pltpu.VMEM)
    smem = pl.BlockSpec(memory_space=pltpu.SMEM)
    levels = ncol.bit_length() - 1
    return pl.pallas_call(
        functools.partial(kernel, nrow, ncol),
        out_shape=jax.ShapeDtypeStruct((rows, width), jnp.bfloat16),
        in_specs=[smem, smem, smem, vmem, vmem],
        out_specs=vmem,
        scratch_shapes=[
            pltpu.VMEM((rows, depth), jnp.bfloat16),
            pltpu.VMEM((tiles_all, depth, TILE), jnp.bfloat16),
            pltpu.VMEM((tiles_all, rows, TILE), jnp.bfloat16),
            pltpu.VMEM((tiles_all, rows, TILE), jnp.bfloat16),
            pltpu.VMEM((tiles_all, rows, TILE), jnp.bfloat16),
            pltpu.SemaphoreType.DMA((tiles_all,)),
            pltpu.SemaphoreType.DMA((tiles_all,)),
            pltpu.SemaphoreType.DMA((tiles_all,)),
            pltpu.SemaphoreType.DMA((tiles_all,)),
            pltpu.SemaphoreType.DMA((tiles_all, levels)),
            pltpu.SemaphoreType.DMA((tiles_all, levels)),
            pltpu.SemaphoreType.DMA((tiles_all, levels)),
            pltpu.SemaphoreType.DMA((tiles_all, levels)),
        ],
        compiler_params=pltpu.CompilerParams(
            collective_id=0, has_side_effects=True, vmem_limit_bytes=48 * 1024 * 1024),
        cost_estimate=pl.CostEstimate(
            flops=2 * rows * depth * tiles_all * TILE, bytes_accessed=4 * rows * depth * 2, transcendentals=0),
    )(amp_occupancy, int_occupancy, owner_map, amplitudes, integrals)


def solution(mesh):
    placed = (P("row", "col"), P("col", "row"), P("row", "col"), P("col", "row"), P())
    body = functools.partial(on_device, mesh.shape["row"], mesh.shape["col"])
    return jax.shard_map(body, mesh=mesh, in_specs=placed, out_specs=P("row", "col"), check_vma=False)
```

time: 117 us -> 103 us (0.88)
  Pallas kernels: 113 us -> 98.5 us
    pallas_call x1, Pallas kernels: 113 us -> 98.5 us  [on_device(): pl.pallas_call(functools.partial(kernel, nrow, ncol), out_shape=jax.Shape...]
where the time goes in v2:
time: 103 us
  Pallas kernels  98.5 us (96%)
  local copies, waits for them, and re-layouts  4.21 us (4%)
    pallas_call x1, Pallas kernels, on_device(): pl.pallas_call(functools.partial(kernel, nrow, ncol), out_shape=jax.Shape...  98.5 us
    unnamed x10, local copies, waits for them, and re-layouts  4.21 us

profile of v2, /device:TPU:0, one launch (start us, length us, event | category | flops | bytes accessed | tf_op | source)
XLA Modules:
  0.0 102.7 jit_solution(3863944817527673257)
XLA Ops:
  0.0 0.0 copy-start.3
  0.0 0.0 copy-start.2
  0.0 0.8 copy.6.int_occ
  0.8 0.0 copy-done.3
  0.8 0.0 copy-done.2
  0.8 0.0 copy-start
  0.8 1.2 %copy-done = bf16[512,1024]{1,0:T(8,128)(2,1)S(1)} copy-done((bf16[512,1024]{1,0:T(8,128)(2,1)S(1)}, bf16[512,1024]{1,0:T(8,128)(2,1)}, u32[]{:S(2)}) %copy-start) | copy-done | bytes 1048600
  2.0 0.0 copy-start.1
  2.0 1.2 %copy-done.1 = bf16[1024,512]{1,0:T(8,128)(2,1)S(1)} copy-done((bf16[1024,512]{1,0:T(8,128)(2,1)S(1)}, bf16[1024,512]{1,0:T(8,128)(2,1)}, u32[]{:S(2)}) %copy-start.1) | copy-done | bytes 1048600
  3.2 98.5 %shard_map.55 = bf16[512,1024]{1,0:T(8,128)(2,1)S(1)} custom-call(s32[4,8]{1,0:T(4,128)S(1)} %copy-done.2, s32[8,4]{1,0:T(8,128)S(1)} %copy.6.int_occ, s32[32]{0:T(128)S(1)} %copy-done.3, bf16[512,1024]{1,0:T(8,128)(2,1)S(1)} %copy-done, bf16[1024,512]{1,0:T(8,128)(2,1)S(1)} %copy-done.1), custom_call_target="tpu_custom_call" | custom-call | flops 4294967296 | bytes 4194304 | tf_op jit(solution)/shard_map/pallas_call | solution.py:230
  101.7 1.0 copy.8
Async XLA Ops:
  0.0 0.8 copy-start.3
  0.0 0.8 copy-start.2
  0.8 1.2 %copy-start = (bf16[512,1024]{1,0:T(8,128)(2,1)S(1)}, bf16[512,1024]{1,0:T(8,128)(2,1)}, u32[]{:S(2)}) copy-start(bf16[512,1024]{1,0:T(8,128)(2,1)} %amp.1) | copy-start | bytes 3145732
  2.0 1.2 %copy-start.1 = (bf16[1024,512]{1,0:T(8,128)(2,1)S(1)}, bf16[1024,512]{1,0:T(8,128)(2,1)}, u32[]{:S(2)}) copy-start(bf16[1024,512]{1,0:T(8,128)(2,1)} %integ.1) | copy-start | bytes 3145732

commit v3 on v2

--- a/solution.py
+++ b/solution.py
@@ -9,7 +9,7 @@
 
 TILE = 128
 CORES = 2
-LAG = 2
+END_LAG, INNER_LAG = 1, 3
 MESH = pl.DeviceIdType.MESH
 
 
@@ -92,6 +92,8 @@
 
     levels = len(order[0])
     units = (nz - 1) * tiles
+    inner = has_left.astype(jnp.int32) * has_right.astype(jnp.int32)
+    lag = END_LAG + (INNER_LAG - END_LAG) * inner
 
     def low(h, level):
         at = 0
@@ -148,8 +150,8 @@
                 if level > 0:
                     up(h, level - 1, tile).start()
 
-    def sides(n, lag, action):
-        at = n - lag
+    def sides(n, behind, action):
+        at = n - behind
         step, j = 1 + at // tiles, lax.rem(at, tiles)
         inside = (at >= 0) & (at < units)
 
@@ -190,12 +192,12 @@
 
             hop(from_right, twin_send, twin).start()
 
-    @pl.loop(0, units + LAG * 2 * levels + 1)
+    @pl.loop(0, units + INNER_LAG * 2 * levels + 1)
     def _(n):
         forward(n)
         sides(n, 0, multiply)
         for stage in range(2 * levels):
-            sides(n, LAG * (stage + 1), functools.partial(advance, stage))
+            sides(n, lag * (stage + 1), functools.partial(advance, stage))
 
     for t in range(per_col):
         out[:, t * TILE:(t + 1) * TILE] = full[owner[col * per_col + t]]

time: 103 us -> 98.3 us (0.954); the launches traced: 103 us -> 96.8 us
  Pallas kernels: 98.5 us -> 92.6 us
    pallas_call x1, Pallas kernels: 98.5 us -> 92.6 us  [on_device(): pl.pallas_call(functools.partial(kernel, nrow, ncol), out_shape=jax.Shape...]
where the time goes in v3:
time: 98.3 us; the launch traced here: 96.8 us
  Pallas kernels  92.6 us (94%)
  local copies, waits for them, and re-layouts  4.21 us (4%)
    pallas_call x1, Pallas kernels, on_device(): pl.pallas_call(functools.partial(kernel, nrow, ncol), out_shape=jax.Shape...  92.6 us
    unnamed x10, local copies, waits for them, and re-layouts  4.21 us

profile of v3, /device:TPU:0, one launch (start us, length us, event | category | flops | bytes accessed | tf_op | source)
XLA Modules:
  0.0 96.8 jit_solution(16022619743272250506)
XLA Ops:
  0.0 0.0 copy-start.3
  0.0 0.0 copy-start.2
  0.0 0.8 copy.6.int_occ
  0.8 0.0 copy-done.3
  0.8 0.0 copy-done.2
  0.8 0.0 copy-start
  0.8 1.2 %copy-done = bf16[512,1024]{1,0:T(8,128)(2,1)S(1)} copy-done((bf16[512,1024]{1,0:T(8,128)(2,1)S(1)}, bf16[512,1024]{1,0:T(8,128)(2,1)}, u32[]{:S(2)}) %copy-start) | copy-done | bytes 1048600
  2.0 0.0 copy-start.1
  2.0 1.2 %copy-done.1 = bf16[1024,512]{1,0:T(8,128)(2,1)S(1)} copy-done((bf16[1024,512]{1,0:T(8,128)(2,1)S(1)}, bf16[1024,512]{1,0:T(8,128)(2,1)}, u32[]{:S(2)}) %copy-start.1) | copy-done | bytes 1048600
  3.2 92.6 %shard_map.55 = bf16[512,1024]{1,0:T(8,128)(2,1)S(1)} custom-call(s32[4,8]{1,0:T(4,128)S(1)} %copy-done.2, s32[8,4]{1,0:T(8,128)S(1)} %copy.6.int_occ, s32[32]{0:T(128)S(1)} %copy-done.3, bf16[512,1024]{1,0:T(8,128)(2,1)S(1)} %copy-done, bf16[1024,512]{1,0:T(8,128)(2,1)S(1)} %copy-done.1), custom_call_target="tpu_custom_call" | custom-call | flops 4294967296 | bytes 4194304 | tf_op jit(solution)/shard_map/pallas_call | solution.py:232
  95.9 1.0 %copy.8 = bf16[512,1024]{1,0:T(8,128)(2,1)} copy(bf16[512,1024]{1,0:T(8,128)(2,1)S(1)} %shard_map.55) | data formatting | bytes 2097152
Async XLA Ops:
  0.0 0.8 copy-start.3
  0.0 0.8 copy-start.2
  0.8 1.2 %copy-start = (bf16[512,1024]{1,0:T(8,128)(2,1)S(1)}, bf16[512,1024]{1,0:T(8,128)(2,1)}, u32[]{:S(2)}) copy-start(bf16[512,1024]{1,0:T(8,128)(2,1)} %amp.1) | copy-start | bytes 3145732
  2.0 1.2 %copy-start.1 = (bf16[1024,512]{1,0:T(8,128)(2,1)S(1)}, bf16[1024,512]{1,0:T(8,128)(2,1)}, u32[]{:S(2)}) copy-start(bf16[1024,512]{1,0:T(8,128)(2,1)} %integ.1) | copy-start | bytes 3145732

commit v4 on v3

--- a/solution.py
+++ b/solution.py
@@ -9,7 +9,7 @@
 
 TILE = 128
 CORES = 2
-END_LAG, INNER_LAG = 1, 3
+END_LAG, INNER_LAG = 1, 2
 MESH = pl.DeviceIdType.MESH
 
 
@@ -27,9 +27,19 @@
     return (bits, bits[::-1])
 
 
+def early_rows(rows, ncol):
+    unit = 16 * ncol
+    return max(unit, rows * 3 // 4 // unit * unit)
+
+
+def first_stage(offset, order):
+    return next(i for i, bit in enumerate(order) if offset & bit)
+
+
 def kernel(nrow, ncol, amp_occ, int_occ, owner, amp, integ, out,
            masked, gath, part, landed, full, recv, right_send, left_send, twin_send,
-           down_send, down_recv, up_send, up_recv):
+           down_send, down_recv, up_send, up_recv,
+           late, late_landed, late_send, late_recv):
     nz = nrow // CORES
     row, col = lax.axis_index("row"), lax.axis_index("col")
     z, core = row // CORES, lax.rem(row, CORES)
@@ -91,6 +101,8 @@
             masked[i * TILE:(i + 1) * TILE, k * TILE:(k + 1) * TILE] = block.astype(jnp.bfloat16)
 
     levels = len(order[0])
+    early = part.shape[1]
+    half = (nrows - early) // 2
     units = (nz - 1) * tiles
     inner = has_left.astype(jnp.int32) * has_right.astype(jnp.int32)
     lag = END_LAG + (INNER_LAG - END_LAG) * inner
@@ -98,17 +110,17 @@
     def low(h, level):
         at = 0
         for k in range(level):
-            at = at + lax.rem(col // order[h][k], 2) * (nrows >> (k + 1))
+            at = at + lax.rem(col // order[h][k], 2) * (early >> (k + 1))
         return at
 
     def span(h, level):
-        return pl.ds(pl.multiple_of(low(h, level), nrows >> level), nrows >> level)
+        return pl.ds(pl.multiple_of(low(h, level), early >> level), early >> level)
 
     def slot(level):
-        return pl.ds(nrows - (nrows >> level), nrows >> (level + 1))
+        return pl.ds(early - (early >> level), early >> (level + 1))
 
     def down(h, level, tile):
-        size = nrows >> (level + 1)
+        size = early >> (level + 1)
         start = low(h, level) + (1 - lax.rem(col // order[h][level], 2)) * size
         return pltpu.make_async_remote_copy(
             src_ref=part.at[tile, pl.ds(pl.multiple_of(start, size), size), :],
@@ -126,7 +138,7 @@
         pair = [(block * CORES + c) * tiles + j for c in range(CORES)]
         hop((block * CORES + (CORES - 1) - core) * tiles + j, twin_send, twin).wait_recv()
         right = jnp.concatenate([gath[tile] for tile in pair], axis=1)
-        value = jnp.dot(masked[...], right, preferred_element_type=jnp.float32).astype(jnp.bfloat16)
+        value = jnp.dot(masked[:early, :], right, preferred_element_type=jnp.float32).astype(jnp.bfloat16)
         for h, tile in enumerate(pair):
             part[tile] = value[:, h * TILE:(h + 1) * TILE]
             down(h, 0, tile).start()
@@ -192,15 +204,72 @@
 
             hop(from_right, twin_send, twin).start()
 
-    @pl.loop(0, units + INNER_LAG * 2 * levels + 1)
+    group = 2 if per_col % 2 == 0 else 1
+
+    def multiply_late(offset):
+        base = flip(col, offset) * per_col
+
+        @pl.loop(0, per_col // group)
+        def _(i):
+            right = [gath[owner[base + i * group + p]] for p in range(group)]
+            right = right[0] if group == 1 else jnp.concatenate(right, axis=1)
+            value = jnp.dot(masked[early:, :], right, preferred_element_type=jnp.float32)
+            at = pl.multiple_of(i * group * TILE, group * TILE)
+            late[offset, :, pl.ds(at, group * TILE)] = value.astype(jnp.bfloat16)
+
+    place = {}
+    for h in range(2):
+        for stage in range(levels):
+            for offset in range(ncol):
+                if not any(offset & bit for bit in order[h][:stage + 1]):
+                    place[h, stage, offset] = len(place)
+
+    def late_hop(h, offset):
+        stage = first_stage(offset, order[h])
+        bit = order[h][stage]
+        there = place[h, stage, offset ^ bit]
+        return pltpu.make_async_remote_copy(
+            src_ref=late.at[offset, pl.ds(h * half, half), :], dst_ref=late_landed.at[there],
+            send_sem=late_send.at[there], recv_sem=late_recv.at[there],
+            device_id={"col": flip(col, bit)}, device_id_type=MESH)
+
+    def late_total(h, stages, offset):
+        value = late[offset, h * half:(h + 1) * half, :].astype(jnp.float32)
+        for stage in range(stages):
+            late_hop(h, offset ^ order[h][stage]).wait_recv()
+            value += late_landed[place[h, stage, offset]].astype(jnp.float32)
+        return value.astype(jnp.bfloat16)
+
+    @pl.loop(0, units)
     def _(n):
         forward(n)
         sides(n, 0, multiply)
         for stage in range(2 * levels):
             sides(n, lag * (stage + 1), functools.partial(advance, stage))
 
+    for offset in range(ncol - 1, -1, -1):
+        multiply_late(offset)
+        for h in range(2):
+            if offset and first_stage(offset, order[h]) == 0:
+                late_hop(h, offset).start()
+
+    @pl.loop(units, units + INNER_LAG * 2 * levels + 1)
+    def _(n):
+        for stage in range(2 * levels):
+            sides(n, lag * (stage + 1), functools.partial(advance, stage))
+
+    for stage in range(1, levels):
+        for h in range(2):
+            for offset in range(ncol - 1, 0, -1):
+                if first_stage(offset, order[h]) == stage:
+                    late[offset, h * half:(h + 1) * half, :] = late_total(h, stage, offset)
+                    late_hop(h, offset).start()
     for t in range(per_col):
-        out[:, t * TILE:(t + 1) * TILE] = full[owner[col * per_col + t]]
+        out[:early, t * TILE:(t + 1) * TILE] = full[owner[col * per_col + t]]
+    for h in range(2):
+        out[early + h * half:early + (h + 1) * half, :] = late_total(h, levels, 0)
+        for offset in range(1, ncol):
+            late_hop(h, offset).wait_send()
 
     @pl.loop(0, nz * tiles)
     def _(n):
@@ -226,6 +295,8 @@
     rows, depth = amplitudes.shape
     tiles_all = nrow * integrals.shape[1] // TILE
     width = tiles_all * TILE // ncol
+    early = early_rows(rows, ncol)
+    places = 2 * (ncol - 1)
     vmem = pl.BlockSpec(memory_space=pltpu.VMEM)
     smem = pl.BlockSpec(memory_space=pltpu.SMEM)
     levels = ncol.bit_length() - 1
@@ -237,9 +308,9 @@
         scratch_shapes=[
             pltpu.VMEM((rows, depth), jnp.bfloat16),
             pltpu.VMEM((tiles_all, depth, TILE), jnp.bfloat16),
-            pltpu.VMEM((tiles_all, rows, TILE), jnp.bfloat16),
-            pltpu.VMEM((tiles_all, rows, TILE), jnp.bfloat16),
-            pltpu.VMEM((tiles_all, rows, TILE), jnp.bfloat16),
+            pltpu.VMEM((tiles_all, early, TILE), jnp.bfloat16),
+            pltpu.VMEM((tiles_all, early, TILE), jnp.bfloat16),
+            pltpu.VMEM((tiles_all, early, TILE), jnp.bfloat16),
             pltpu.SemaphoreType.DMA((tiles_all,)),
             pltpu.SemaphoreType.DMA((tiles_all,)),
             pltpu.SemaphoreType.DMA((tiles_all,)),
@@ -248,6 +319,10 @@
             pltpu.SemaphoreType.DMA((tiles_all, levels)),
             pltpu.SemaphoreType.DMA((tiles_all, levels)),
             pltpu.SemaphoreType.DMA((tiles_all, levels)),
+            pltpu.VMEM((ncol, rows - early, width), jnp.bfloat16),
+            pltpu.VMEM((places, (rows - early) // 2, width), jnp.bfloat16),
+            pltpu.SemaphoreType.DMA((places,)),
+            pltpu.SemaphoreType.DMA((places,)),
         ],
         compiler_params=pltpu.CompilerParams(
             collective_id=0, has_side_effects=True, vmem_limit_bytes=48 * 1024 * 1024),

time: 98.3 us -> 105 us (1.068); the launches traced: 96.8 us -> 105 us
  Pallas kernels: 92.6 us -> 101 us
    pallas_call x1, Pallas kernels: 92.6 us -> 101 us  [on_device(): pl.pallas_call(functools.partial(kernel, nrow, ncol), out_shape=jax.Shape...]
where the time goes in v4:
time: 105 us
  Pallas kernels  101 us (96%)
  local copies, waits for them, and re-layouts  4.21 us (4%)
    pallas_call x1, Pallas kernels, on_device(): pl.pallas_call(functools.partial(kernel, nrow, ncol), out_shape=jax.Shape...  101 us
    unnamed x10, local copies, waits for them, and re-layouts  4.21 us

profile of v4, /device:TPU:0, one launch (start us, length us, event | category | flops | bytes accessed | tf_op | source)
XLA Modules:
  0.0 104.8 jit_solution(18086092133108282663)
XLA Ops:
  0.0 0.0 copy-start.3
  0.0 0.0 copy-start.2
  0.0 0.8 copy.6.int_occ
  0.8 0.0 copy-done.3
  0.8 0.0 copy-done.2
  0.8 0.0 copy-start
  0.8 1.2 %copy-done = bf16[512,1024]{1,0:T(8,128)(2,1)S(1)} copy-done((bf16[512,1024]{1,0:T(8,128)(2,1)S(1)}, bf16[512,1024]{1,0:T(8,128)(2,1)}, u32[]{:S(2)}) %copy-start) | copy-done | bytes 1048600
  2.0 0.0 copy-start.1
  2.0 1.2 %copy-done.1 = bf16[1024,512]{1,0:T(8,128)(2,1)S(1)} copy-done((bf16[1024,512]{1,0:T(8,128)(2,1)S(1)}, bf16[1024,512]{1,0:T(8,128)(2,1)}, u32[]{:S(2)}) %copy-start.1) | copy-done | bytes 1048600
  3.2 100.6 %shard_map.55 = bf16[512,1024]{1,0:T(8,128)(2,1)S(1)} custom-call(s32[4,8]{1,0:T(4,128)S(1)} %copy-done.2, s32[8,4]{1,0:T(8,128)S(1)} %copy.6.int_occ, s32[32]{0:T(128)S(1)} %copy-done.3, bf16[512,1024]{1,0:T(8,128)(2,1)S(1)} %copy-done, bf16[1024,512]{1,0:T(8,128)(2,1)S(1)} %copy-done.1), custom_call_target="tpu_custom_call" | custom-call | flops 4294967296 | bytes 4194304 | tf_op jit(solution)/shard_map/pallas_call | solution.py:303
  103.8 1.0 copy.8
Async XLA Ops:
  0.0 0.8 copy-start.3
  0.0 0.8 copy-start.2
  0.8 1.2 %copy-start = (bf16[512,1024]{1,0:T(8,128)(2,1)S(1)}, bf16[512,1024]{1,0:T(8,128)(2,1)}, u32[]{:S(2)}) copy-start(bf16[512,1024]{1,0:T(8,128)(2,1)} %amp.1) | copy-start | bytes 3145732
  2.0 1.2 %copy-start.1 = (bf16[1024,512]{1,0:T(8,128)(2,1)S(1)}, bf16[1024,512]{1,0:T(8,128)(2,1)}, u32[]{:S(2)}) copy-start(bf16[1024,512]{1,0:T(8,128)(2,1)} %integ.1) | copy-start | bytes 3145732

commit v5 on v3

--- a/solution.py
+++ b/solution.py
@@ -9,7 +9,7 @@
 
 TILE = 128
 CORES = 2
-END_LAG, INNER_LAG = 1, 3
+END_LAG, INNER_LAG = 1, 2
 MESH = pl.DeviceIdType.MESH
 
 
@@ -155,9 +155,9 @@
         step, j = 1 + at // tiles, lax.rem(at, tiles)
         inside = (at >= 0) & (at < units)
 
-        @pl.when((at >= 0) & (at < tiles))
-        def _():
-            action(z, at)
+        @pl.when((at >= 0) & (at < 2 * tiles) & (lax.rem(at, 2) == 0))
+        def _():
+            action(z, at // 2)
 
         @pl.when(inside & (z - step >= 0))
         def _():
@@ -192,7 +192,7 @@
 
             hop(from_right, twin_send, twin).start()
 
-    @pl.loop(0, units + INNER_LAG * 2 * levels + 1)
+    @pl.loop(0, max(units, 2 * tiles) + INNER_LAG * 2 * levels + 1)
     def _(n):
         forward(n)
         sides(n, 0, multiply)

time: 98.3 us -> 99.5 us (1.012); the launches traced: 96.8 us -> 99.3 us
  Pallas kernels: 92.6 us -> 95.1 us
    pallas_call x1, Pallas kernels: 92.6 us -> 95.1 us  [on_device(): pl.pallas_call(functools.partial(kernel, nrow, ncol), out_shape=jax.Shape...]
where the time goes in v5:
time: 99.5 us; the launch traced here: 99.3 us
  Pallas kernels  95.1 us (96%)
  local copies, waits for them, and re-layouts  4.21 us (4%)
    pallas_call x1, Pallas kernels, on_device(): pl.pallas_call(functools.partial(kernel, nrow, ncol), out_shape=jax.Shape...  95.1 us
    unnamed x10, local copies, waits for them, and re-layouts  4.21 us

profile of v5, /device:TPU:0, one launch (start us, length us, event | category | flops | bytes accessed | tf_op | source)
XLA Modules:
  0.0 99.3 jit_solution(17482696919032376540)
XLA Ops:
  0.0 0.0 copy-start.3
  0.0 0.0 copy-start.2
  0.0 0.8 copy.6.int_occ
  0.8 0.0 copy-done.3
  0.8 0.0 copy-done.2
  0.8 0.0 copy-start
  0.8 1.2 %copy-done = bf16[512,1024]{1,0:T(8,128)(2,1)S(1)} copy-done((bf16[512,1024]{1,0:T(8,128)(2,1)S(1)}, bf16[512,1024]{1,0:T(8,128)(2,1)}, u32[]{:S(2)}) %copy-start) | copy-done | bytes 1048600
  2.0 0.0 copy-start.1
  2.0 1.2 %copy-done.1 = bf16[1024,512]{1,0:T(8,128)(2,1)S(1)} copy-done((bf16[1024,512]{1,0:T(8,128)(2,1)S(1)}, bf16[1024,512]{1,0:T(8,128)(2,1)}, u32[]{:S(2)}) %copy-start.1) | copy-done | bytes 1048600
  3.2 95.1 %shard_map.55 = bf16[512,1024]{1,0:T(8,128)(2,1)S(1)} custom-call(s32[4,8]{1,0:T(4,128)S(1)} %copy-done.2, s32[8,4]{1,0:T(8,128)S(1)} %copy.6.int_occ, s32[32]{0:T(128)S(1)} %copy-done.3, bf16[512,1024]{1,0:T(8,128)(2,1)S(1)} %copy-done, bf16[1024,512]{1,0:T(8,128)(2,1)S(1)} %copy-done.1), custom_call_target="tpu_custom_call" | custom-call | flops 4294967296 | bytes 4194304 | tf_op jit(solution)/shard_map/pallas_call | solution.py:232
  98.3 1.0 copy.8
Async XLA Ops:
  0.0 0.8 copy-start.3
  0.0 0.8 copy-start.2
  0.8 1.2 %copy-start = (bf16[512,1024]{1,0:T(8,128)(2,1)S(1)}, bf16[512,1024]{1,0:T(8,128)(2,1)}, u32[]{:S(2)}) copy-start(bf16[512,1024]{1,0:T(8,128)(2,1)} %amp.1) | copy-start | bytes 3145732
  2.0 1.2 %copy-start.1 = (bf16[1024,512]{1,0:T(8,128)(2,1)S(1)}, bf16[1024,512]{1,0:T(8,128)(2,1)}, u32[]{:S(2)}) copy-start(bf16[1024,512]{1,0:T(8,128)(2,1)} %integ.1) | copy-start | bytes 3145732

commit v6 on v3

--- a/solution.py
+++ b/solution.py
@@ -9,7 +9,7 @@
 
 TILE = 128
 CORES = 2
-END_LAG, INNER_LAG = 1, 3
+INNER_LAG = 2
 MESH = pl.DeviceIdType.MESH
 
 
@@ -93,7 +93,6 @@
     levels = len(order[0])
     units = (nz - 1) * tiles
     inner = has_left.astype(jnp.int32) * has_right.astype(jnp.int32)
-    lag = END_LAG + (INNER_LAG - END_LAG) * inner
 
     def low(h, level):
         at = 0
@@ -196,8 +195,10 @@
     def _(n):
         forward(n)
         sides(n, 0, multiply)
-        for stage in range(2 * levels):
-            sides(n, lag * (stage + 1), functools.partial(advance, stage))
+        for stage in list(range(1, 2 * levels, 2)) + list(range(0, 2 * levels, 2)):
+            at_end = (stage + 1) // 2
+            behind = at_end + (INNER_LAG * (stage + 1) - at_end) * inner
+            sides(n, behind, functools.partial(advance, stage))
 
     for t in range(per_col):
         out[:, t * TILE:(t + 1) * TILE] = full[owner[col * per_col + t]]

time: 98.3 us -> 109 us (1.11)
  Pallas kernels: 92.6 us -> 104 us
    pallas_call x1, Pallas kernels: 92.6 us -> 104 us  [on_device(): pl.pallas_call(functools.partial(kernel, nrow, ncol), out_shape=jax.Shape...]
where the time goes in v6:
time: 109 us
  Pallas kernels  104 us (95%)
  local copies, waits for them, and re-layouts  4.21 us (4%)
    pallas_call x1, Pallas kernels, on_device(): pl.pallas_call(functools.partial(kernel, nrow, ncol), out_shape=jax.Shape...  104 us
    unnamed x10, local copies, waits for them, and re-layouts  4.21 us

profile of v6, /device:TPU:0, one launch (start us, length us, event | category | flops | bytes accessed | tf_op | source)
XLA Modules:
  0.0 108.6 jit_solution(16548575383415716375)
XLA Ops:
  0.0 0.0 copy-start.3
  0.0 0.0 copy-start.2
  0.0 0.8 copy.6.int_occ
  0.8 0.0 copy-done.3
  0.8 0.0 copy-done.2
  0.8 0.0 copy-start
  0.8 1.2 %copy-done = bf16[512,1024]{1,0:T(8,128)(2,1)S(1)} copy-done((bf16[512,1024]{1,0:T(8,128)(2,1)S(1)}, bf16[512,1024]{1,0:T(8,128)(2,1)}, u32[]{:S(2)}) %copy-start) | copy-done | bytes 1048600
  2.0 0.0 copy-start.1
  2.0 1.2 %copy-done.1 = bf16[1024,512]{1,0:T(8,128)(2,1)S(1)} copy-done((bf16[1024,512]{1,0:T(8,128)(2,1)S(1)}, bf16[1024,512]{1,0:T(8,128)(2,1)}, u32[]{:S(2)}) %copy-start.1) | copy-done | bytes 1048600
  3.2 104.4 %shard_map.55 = bf16[512,1024]{1,0:T(8,128)(2,1)S(1)} custom-call(s32[4,8]{1,0:T(4,128)S(1)} %copy-done.2, s32[8,4]{1,0:T(8,128)S(1)} %copy.6.int_occ, s32[32]{0:T(128)S(1)} %copy-done.3, bf16[512,1024]{1,0:T(8,128)(2,1)S(1)} %copy-done, bf16[1024,512]{1,0:T(8,128)(2,1)S(1)} %copy-done.1), custom_call_target="tpu_custom_call" | custom-call | flops 4294967296 | bytes 4194304 | tf_op jit(solution)/shard_map/pallas_call | solution.py:233
  107.6 1.0 copy.8
Async XLA Ops:
  0.0 0.8 copy-start.3
  0.0 0.8 copy-start.2
  0.8 1.2 %copy-start = (bf16[512,1024]{1,0:T(8,128)(2,1)S(1)}, bf16[512,1024]{1,0:T(8,128)(2,1)}, u32[]{:S(2)}) copy-start(bf16[512,1024]{1,0:T(8,128)(2,1)} %amp.1) | copy-start | bytes 3145732
  2.0 1.2 %copy-start.1 = (bf16[1024,512]{1,0:T(8,128)(2,1)S(1)}, bf16[1024,512]{1,0:T(8,128)(2,1)}, u32[]{:S(2)}) copy-start(bf16[1024,512]{1,0:T(8,128)(2,1)} %integ.1) | copy-start | bytes 3145732

commit v7 on v3

--- a/solution.py
+++ b/solution.py
@@ -9,7 +9,7 @@
 
 TILE = 128
 CORES = 2
-END_LAG, INNER_LAG = 1, 3
+END_LAG, INNER_LAG = 1, 2
 MESH = pl.DeviceIdType.MESH
 
 
@@ -192,12 +192,12 @@
 
             hop(from_right, twin_send, twin).start()
 
-    @pl.loop(0, units + INNER_LAG * 2 * levels + 1)
+    @pl.loop(0, units + INNER_LAG * 2 * levels + 2)
     def _(n):
         forward(n)
         sides(n, 0, multiply)
         for stage in range(2 * levels):
-            sides(n, lag * (stage + 1), functools.partial(advance, stage))
+            sides(n, lag * (stage + 1) + inner, functools.partial(advance, stage))
 
     for t in range(per_col):
         out[:, t * TILE:(t + 1) * TILE] = full[owner[col * per_col + t]]

time: 98.3 us -> 97 us (0.987); the launches traced: 96.8 us -> 96.8 us
  no operation moved by 1% of the time
where the time goes in v7:
time: 97 us; the launch traced here: 96.8 us
  Pallas kernels  92.6 us (95%)
  local copies, waits for them, and re-layouts  4.21 us (4%)
    pallas_call x1, Pallas kernels, on_device(): pl.pallas_call(functools.partial(kernel, nrow, ncol), out_shape=jax.Shape...  92.6 us
    unnamed x10, local copies, waits for them, and re-layouts  4.21 us

profile of v7, /device:TPU:0, one launch (start us, length us, event | category | flops | bytes accessed | tf_op | source)
XLA Modules:
  0.0 96.8 jit_solution(6454101100607577062)
XLA Ops:
  0.0 0.0 copy-start.3
  0.0 0.0 copy-start.2
  0.0 0.8 copy.6.int_occ
  0.8 0.0 copy-done.3
  0.8 0.0 copy-done.2
  0.8 0.0 copy-start
  0.8 1.2 %copy-done = bf16[512,1024]{1,0:T(8,128)(2,1)S(1)} copy-done((bf16[512,1024]{1,0:T(8,128)(2,1)S(1)}, bf16[512,1024]{1,0:T(8,128)(2,1)}, u32[]{:S(2)}) %copy-start) | copy-done | bytes 1048600
  2.0 0.0 copy-start.1
  2.0 1.2 %copy-done.1 = bf16[1024,512]{1,0:T(8,128)(2,1)S(1)} copy-done((bf16[1024,512]{1,0:T(8,128)(2,1)S(1)}, bf16[1024,512]{1,0:T(8,128)(2,1)}, u32[]{:S(2)}) %copy-start.1) | copy-done | bytes 1048600
  3.2 92.6 %shard_map.55 = bf16[512,1024]{1,0:T(8,128)(2,1)S(1)} custom-call(s32[4,8]{1,0:T(4,128)S(1)} %copy-done.2, s32[8,4]{1,0:T(8,128)S(1)} %copy.6.int_occ, s32[32]{0:T(128)S(1)} %copy-done.3, bf16[512,1024]{1,0:T(8,128)(2,1)S(1)} %copy-done, bf16[1024,512]{1,0:T(8,128)(2,1)S(1)} %copy-done.1), custom_call_target="tpu_custom_call" | custom-call | flops 4294967296 | bytes 4194304 | tf_op jit(solution)/shard_map/pallas_call | solution.py:232
  95.9 1.0 %copy.8 = bf16[512,1024]{1,0:T(8,128)(2,1)} copy(bf16[512,1024]{1,0:T(8,128)(2,1)S(1)} %shard_map.55) | data formatting | bytes 2097152
Async XLA Ops:
  0.0 0.8 copy-start.3
  0.0 0.8 copy-start.2
  0.8 1.2 %copy-start = (bf16[512,1024]{1,0:T(8,128)(2,1)S(1)}, bf16[512,1024]{1,0:T(8,128)(2,1)}, u32[]{:S(2)}) copy-start(bf16[512,1024]{1,0:T(8,128)(2,1)} %amp.1) | copy-start | bytes 3145732
  2.0 1.2 %copy-start.1 = (bf16[1024,512]{1,0:T(8,128)(2,1)S(1)}, bf16[1024,512]{1,0:T(8,128)(2,1)}, u32[]{:S(2)}) copy-start(bf16[1024,512]{1,0:T(8,128)(2,1)} %integ.1) | copy-start | bytes 3145732
